TPU v7x, 32 devices: a whole 2x2x4 slice. The times are simulated.
32 devices in a mesh: rep: 8 (over z, y), fsdp: 4 (over x, core).
Axes of the slice: x: 2, y: 2, z: 4, core: 2. Of those that a mesh axis runs over, the one named last changes fastest.
Arguments:
- tokens: bfloat16 [16384, 4096], P(('rep', 'fsdp')), may hold values from -6 to 6
- gate_pre: bfloat16 [16384, 768], P(('rep', 'fsdp')), may hold values from -8 to 8
- upstream: bfloat16 [16384, 768], P(('rep', 'fsdp')), may hold values from -6 to 6
- slow: float32 [8, 4096, 768], P('rep', 'fsdp'), may hold values from -6 to 6
- inner_mom: bfloat16 [8, 4096, 768], P('rep', 'fsdp'), may hold values from -6 to 6
- outer_mom: bfloat16 [8, 4096, 768], P('rep', 'fsdp'), may hold values from -3 to 3
- pairing: int32 [8], replicated, may hold values from 0 to 7, as said below
Outputs:
- gate_grad: bfloat16 [16384, 768], P(('rep', 'fsdp'))
- inner_new: bfloat16 [8, 4096, 768], P('rep', 'fsdp')
- outer_new: bfloat16 [8, 4096, 768], P('rep', 'fsdp')
- slow_new: float32 [8, 4096, 768], P('rep', 'fsdp')
Inputs may be any that keep to these rules, and one draw needn't show every extreme that they name: pairing[i] = i XOR p for one p of 1 to 7 shared by all i, so pairing[pairing[i]] = i.
All inputs are finite; a program needn't handle non-finite values.
Results may differ from a plain program's by a relative error of at most 0.009.
Values may be sent and summed in bfloat16 or wider, within the bound.
A program may use at most 128 MiB of HBM per device.

v0:
```python
import functools

import jax
import jax.numpy as jnp
from jax import lax
from jax.experimental import pallas as pl
from jax.experimental.pallas import tpu as pltpu
from jax.sharding import PartitionSpec as P

inner_beta = 0.9
inner_rate = 0.5
outer_mu = 0.9
outer_rate = 0.7

MESH = pl.DeviceIdType.MESH
F32 = jnp.float32
BF16 = jnp.bfloat16
CHUNK = 256
STRIP = 16
GATE_PIECES = 4


def flipped(index, mask):
    out = index
    for bit in range(mask.bit_length()):
        if mask >> bit & 1:
            out = out + (1 - 2 * lax.rem(lax.div(index, 1 << bit), 2)) * (1 << bit)
    return out


def kernel(
    xor, n, far, scale,
    tok_hbm, gate_hbm, ups_hbm, slow_hbm, imom_hbm, omom_hbm,
    gate_grad, inner_new, outer_new, slow_new,
    tok, gate, ups, slow, imom, omom,
    fast, grad, s1_out, s1_in, s2_out, s2_in, own, og_out, og_in, slow_in, acc, factor,
    in_sem, slow_sem, s1_sem, s2_sem, ag_sem, fw_sem, og_sem,
):
    rows = slow.shape[0]
    piece = min(CHUNK, rows)
    count = rows // piece
    early = count // 2
    chips = n // 2
    rep, me = lax.axis_index("rep"), lax.axis_index("fsdp")
    chip, core = lax.div(me, 2), lax.rem(me, 2)
    sibling = (rep, chip * 2 + 1 - core)
    partner = (flipped(rep, xor), me)

    def ahead(j):
        return lax.rem(chip + j, chips)

    def behind(j):
        return lax.rem(chip + chips - j, chips)

    def part(k):
        return pl.ds(pl.multiple_of(k * piece, piece), piece)

    def weight_part(block, k):
        start = pl.multiple_of(block * rows + k * piece, piece)
        return lax.dot_general(
            tok[:, pl.ds(start, piece)], grad[...], (((0,), (0,)), ((), ())),
            preferred_element_type=F32,
        )

    def remote(src, dst, sems, slot, device):
        return pltpu.make_async_remote_copy(
            src_ref=src, dst_ref=dst, send_sem=sems.at[0, slot], recv_sem=sems.at[1, slot],
            device_id=device, device_id_type=MESH,
        )

    def s1_copy(j, k):
        return remote(s1_out.at[j, part(k)], s1_in.at[j, part(k)], s1_sem, j * count + k, sibling)

    def s2_copy(j, k):
        return remote(
            s2_out.at[j - 1, part(k)], s2_in.at[j - 1, part(k)], s2_sem, (j - 1) * count + k,
            (rep, ahead(j) * 2 + core),
        )

    def ag_copy(j, k, block):
        return remote(
            fast.at[block, part(k)], fast.at[block, part(k)], ag_sem, (j - 1) * count + k,
            (rep, ahead(j) * 2 + core),
        )

    def fw_copy(j, k, block):
        return remote(
            fast.at[block, part(k)], fast.at[block, part(k)], fw_sem, j * count + k, sibling
        )

    def og_copy(k):
        return remote(og_out.at[part(k)], og_in.at[part(k)], og_sem, k, partner)

    def loop(stop, body, start=0):
        def step(i, carry):
            body(i)
            return carry

        lax.fori_loop(start, stop, step, 0)

    def slow_load(k):
        return pltpu.make_async_copy(slow_hbm.at[part(k)], slow.at[part(k)], in_sem.at[5 + k])

    def load(i):
        src, dst = ((gate_hbm, gate), (ups_hbm, ups), (tok_hbm, tok), (imom_hbm, imom), (omom_hbm, omom))[i]
        return pltpu.make_async_copy(src, dst, in_sem.at[i])

    tall = gate_grad.shape[0] // GATE_PIECES

    barrier = pltpu.get_barrier_semaphore()
    pl.semaphore_signal(barrier, inc=1, device_id=sibling, device_id_type=MESH)
    pl.semaphore_signal(barrier, inc=1, device_id=partner, device_id_type=MESH)
    for j in range(1, chips):
        pl.semaphore_signal(
            barrier, inc=1, device_id=(rep, ahead(j) * 2 + core), device_id_type=MESH
        )

    loop(count, lambda k: slow_load(k).start())
    for i in range(5):
        load(i).start()

    def cast_slow(k):
        slow_load(k).wait()

        def strip(i):
            at = pl.ds(pl.multiple_of(k * piece + i * STRIP, STRIP), STRIP)
            fast[me, at, :] = slow[at, :].astype(BF16)

        loop(piece // STRIP, strip)

    def slow_copy(k):
        return remote(fast.at[me, part(k)], slow_in.at[part(k)], slow_sem, k, partner)

    def gather_part(k):
        for j in range(1, chips):
            ag_copy(j, k, me).start()

    cast_slow(0)
    pl.semaphore_wait(barrier, chips + 1)

    def send_slow(k):
        slow_copy(k).start()

    send_slow(0)
    if early:
        gather_part(0)

    def cast_and_send(k):
        cast_slow(k)
        send_slow(k)

    def cast_and_gather(k):
        cast_and_send(k)
        gather_part(k)

    loop(early, cast_and_gather, start=1)
    loop(count, cast_and_send, start=max(early, 1))
    load(0).wait()
    load(1).wait()

    def make_grad(i):
        at = pl.ds(pl.multiple_of(i * STRIP, STRIP), STRIP)
        g, u = gate[at, :].astype(F32), ups[at, :].astype(F32)
        s = jax.nn.sigmoid(g)
        grad[at, :] = (u * g * s).astype(BF16)
        factor[at, :] = u * scale * s * (1.0 + g * (1.0 - s))

    loop(grad.shape[0] // STRIP, make_grad)

    load(2).wait()

    def first_hop(j, k):
        block = ahead(j) * 2 + 1 - core
        s1_out[j, part(k), :] = weight_part(block, k).astype(BF16)
        s1_copy(j, k).start()

    def second_hop(j, k):
        mine = weight_part(ahead(j) * 2 + core, k)
        s1_copy(j, k).wait_recv()
        s2_out[j - 1, part(k), :] = (mine + s1_in[j, part(k), :].astype(F32)).astype(BF16)
        s2_copy(j, k).start()

    remote_parts = (chips - 1) * count
    loop(remote_parts, lambda t: first_hop(lax.div(t, count) + 1, lax.rem(t, count)))
    loop(remote_parts, lambda t: second_hop(lax.div(t, count) + 1, lax.rem(t, count)))
    loop(count, lambda k: first_hop(0, k))
    loop(count, lambda k: fw_copy(0, k, me).start())

    def own_part(k):
        own[part(k), :] = weight_part(me, k)

    loop(count, own_part)

    def own_sum(k):
        s1_copy(0, k).wait_recv()
        for j in range(1, chips):
            s2_copy(j, k).wait_recv()

        def strip(i):
            at = pl.ds(pl.multiple_of(k * piece + i * STRIP, STRIP), STRIP)
            total = own[at, :] + s1_in[0, at, :].astype(F32)
            for j in range(1, chips):
                total = total + s2_in[j - 1, at, :].astype(F32)
            new = (inner_beta * imom[at, :].astype(F32) + total * scale).astype(BF16)
            inner_new[at, :] = new
            og = slow[at, :] - (fast[me, at, :].astype(F32) - inner_rate * new.astype(F32))
            own[at, :] = og
            og_out[at, :] = og.astype(BF16)

        loop(piece // STRIP, strip)
        og_copy(k).start()

    def up_part(block, k, first):
        start = pl.multiple_of(block * rows + k * piece, piece)
        value = jnp.dot(
            tok[:, pl.ds(start, piece)], fast[block, part(k), :], preferred_element_type=F32
        )
        acc[...] = value if first else acc[...] + value

    up_part(me, 0, True)
    loop(count, lambda k: up_part(me, k, False), start=1)

    def sibling_part(k):
        fw_copy(0, k, me).wait_recv()
        up_part(chip * 2 + 1 - core, k, False)

    loop(count, sibling_part)

    def gathered(j, k, last=False):
        block = behind(j) * 2 + core
        ag_copy(j, k, block).wait_recv()
        fw_copy(j, k, block).start()
        up_part(block, k, False)
        fw_copy(j, k, block).wait_recv()
        if not last:
            up_part(behind(j) * 2 + 1 - core, k, False)

    for j in range(1, chips):
        loop(early, functools.partial(gathered, j))
    load(3).wait()
    loop(count - 1, own_sum)
    loop(min(early + 1, count), gather_part, start=early)
    own_sum(count - 1)
    loop(count, gather_part, start=early + 1)

    def finish_weights():
        load(4).wait()

        def finish(k):
            slow_copy(k).wait_recv()
            og_copy(k).wait_recv()

            def strip(i):
                at = pl.ds(pl.multiple_of(k * piece + i * STRIP, STRIP), STRIP)
                mean_slow = 0.5 * (slow[at, :] + slow_in[at, :].astype(F32))
                mean_grad = 0.5 * (own[at, :] + og_in[at, :].astype(F32))
                new = (outer_mu * omom[at, :].astype(F32) + mean_grad).astype(BF16)
                outer_new[at, :] = new
                slow_new[at, :] = mean_slow - outer_rate * (
                    mean_grad + outer_mu * new.astype(F32)
                )

            loop(piece // STRIP, strip)

        loop(count, finish)

    def finish_gate():
        for j in range(1, chips - 1):
            loop(count, functools.partial(gathered, j), start=early)
        loop(count - 1, functools.partial(gathered, chips - 1), start=early)
        gathered(chips - 1, count - 1, last=True)
        block = behind(chips - 1) * 2 + 1 - core
        start = pl.multiple_of(block * rows + (count - 1) * piece, piece)

        def gate_piece(k):
            at = pl.ds(pl.multiple_of(k * tall, tall), tall)
            value = jnp.dot(
                tok[at, pl.ds(start, piece)], fast[block, part(count - 1), :],
                preferred_element_type=F32,
            )
            gate_grad[at, :] = ((acc[at, :] + value) * factor[at, :]).astype(BF16)

        loop(GATE_PIECES, gate_piece)

    if far:
        finish_gate()
        finish_weights()
    else:
        finish_weights()
        finish_gate()

    def drain(k):
        slow_copy(k).wait_send()
        og_copy(k).wait_send()
        for j in range(chips):
            s1_copy(j, k).wait_send()
            fw_copy(j, k, behind(j) * 2 + core).wait_send()
        for j in range(1, chips):
            s2_copy(j, k).wait_send()
            ag_copy(j, k, me).wait_send()

    loop(count, drain)


def outer_step(xor, n_rep, n, scale, tokens, gate_pre, upstream, slow, inner_mom, outer_mom):
    rows, cols = slow.shape
    held = tokens.shape[0]
    chips = n // 2
    count = rows // min(CHUNK, rows)
    hbm = pl.BlockSpec(memory_space=pl.ANY)
    flops = 4 * held * tokens.shape[1] * cols
    return pl.pallas_call(
        functools.partial(kernel, xor, n, 2 * xor >= n_rep, scale),
        out_shape=(
            pltpu.VMEM((held, cols), BF16),
            pltpu.VMEM((rows, cols), BF16),
            pltpu.VMEM((rows, cols), BF16),
            pltpu.VMEM((rows, cols), F32),
        ),
        in_specs=[hbm] * 6,
        out_specs=(pl.BlockSpec(memory_space=pltpu.VMEM),) * 4,
        scratch_shapes=[
            pltpu.VMEM(tokens.shape, BF16),
            pltpu.VMEM((held, cols), BF16),
            pltpu.VMEM((held, cols), BF16),
            pltpu.VMEM((rows, cols), F32),
            pltpu.VMEM((rows, cols), BF16),
            pltpu.VMEM((rows, cols), BF16),
            pltpu.VMEM((n, rows, cols), BF16),
            pltpu.VMEM((held, cols), BF16),
            pltpu.VMEM((chips, rows, cols), BF16),
            pltpu.VMEM((chips, rows, cols), BF16),
            pltpu.VMEM((chips - 1, rows, cols), BF16),
            pltpu.VMEM((chips - 1, rows, cols), BF16),
            pltpu.VMEM((rows, cols), F32),
            pltpu.VMEM((rows, cols), BF16),
            pltpu.VMEM((rows, cols), BF16),
            pltpu.VMEM((rows, cols), BF16),
            pltpu.VMEM((held, cols), F32),
            pltpu.VMEM((held, cols), F32),
            pltpu.SemaphoreType.DMA((5 + count,)),
            pltpu.SemaphoreType.DMA((2, count)),
            pltpu.SemaphoreType.DMA((2, chips * count)),
            pltpu.SemaphoreType.DMA((2, (chips - 1) * count)),
            pltpu.SemaphoreType.DMA((2, (chips - 1) * count)),
            pltpu.SemaphoreType.DMA((2, chips * count)),
            pltpu.SemaphoreType.DMA((2, count)),
        ],
        compiler_params=pltpu.CompilerParams(
            collective_id=xor, has_side_effects=True, vmem_limit_bytes=54 * 1024 * 1024
        ),
        cost_estimate=pl.CostEstimate(
            flops=flops, bytes_accessed=2 * tokens.size + 22 * slow.size, transcendentals=0
        ),
    )(tokens, gate_pre, upstream, slow, inner_mom, outer_mom)


def solution(mesh):
    n_rep, n = mesh.shape["rep"], mesh.shape["fsdp"]

    def local(tokens, gate_pre, upstream, slow, inner_mom, outer_mom, pairing):
        scale = float(tokens.shape[1]) ** -0.5
        branches = [
            functools.partial(outer_step, xor, n_rep, n, scale) for xor in range(1, n_rep)
        ]
        gate_grad, inner_new, outer_new, slow_new = lax.switch(
            pairing[0] - 1, branches,
            tokens, gate_pre, upstream, slow[0], inner_mom[0], outer_mom[0],
        )
        return gate_grad, inner_new[None], outer_new[None], slow_new[None]

    rows, weights = P(("rep", "fsdp"), None), P("rep", "fsdp", None)
    return jax.shard_map(
        local,
        mesh=mesh,
        in_specs=(rows, rows, rows, weights, weights, weights, P()),
        out_specs=(rows, weights, weights, weights),
        check_vma=False,
    )
```

profile of v0, /device:TPU:0, one launch (start us, length us, event | category | flops | bytes accessed | tf_op | source)
XLA Modules:
  0.0 148.7 jit_solution(15936269863827050508)
XLA Ops:
  1.3 142.6 %conditional.1 = ((bf16[512,768]{1,0:T(8,128)(2,1)S(1)}, bf16[1024,768]{1,0:T(8,128)(2,1)S(1)}, bf16[1024,768]{1,0:T(8,128)(2,1)S(1)}, f32[1024,768]{1,0:T(8,128)S(1)})) conditional(s32[]{:T(128)} %bitcast, (bf16[512,4096]{1,0:T(8,128)(2,1)}, bf16[512,768]{1,0:T(8,128)(2,1)}, bf16[512,768]{1,0:T(8,128)(2,1)}, ...), branch_computations={%region_0.0_spmd, %region_1.0_spmd, %region_2.0_spmd, %region_3.0_... | conditional | flops 6442450944 | bytes 21495816 | solution.py:366
  1.5 142.0 %branch_3_fun.1 = (bf16[512,768]{1,0:T(8,128)(2,1)S(1)}, bf16[1024,768]{1,0:T(8,128)(2,1)S(1)}, bf16[1024,768]{1,0:T(8,128)(2,1)S(1)}, f32[1024,768]{1,0:T(8,128)S(1)}) custom-call(bf16[512,4096]{1,0:T(8,128)(2,1)} %get-tuple-element.145.tok_hbm, bf16[512,768]{1,0:T(8,128)(2,1)} %get-tuple-element.146.gate_hbm, bf16[512,768]{1,0:T(8,128)(2,1)} %get-tuple-element.147.ups_hbm, ...), custom_call_target="tpu_custom_call" | custom-call | flops 6442450944 | bytes 21495808 | tf_op jit(solution)/shard_map/cond/branch_3_fun/pallas_call | solution.py:312
  143.9 1.7 %copy.46 = f32[1,1024,768]{2,1,0:T(8,128)} copy(f32[1,1024,768]{2,1,0:T(8,128)S(1)} %bitcast.8) | data formatting | bytes 6291456
  145.6 1.1 copy.45
  146.7 0.9 copy.43
  147.6 1.1 copy.44
where the time goes:
time: 149 us
  Pallas kernels  142 us (95%)
  local copies, waits for them, and re-layouts  4.83 us (3%)
    pallas_call x1, Pallas kernels, outer_step(): pl.pallas_call(functools.partial(kernel, xor, n, 2 * xor >= n_rep, scale)...  142 us
    unnamed x4, local copies, waits for them, and re-layouts  4.83 us

commit v1 on v0

--- a/solution.py
+++ b/solution.py
@@ -115,9 +115,7 @@
             barrier, inc=1, device_id=(rep, ahead(j) * 2 + core), device_id_type=MESH
         )
 
-    loop(count, lambda k: slow_load(k).start())
-    for i in range(5):
-        load(i).start()
+    slow_load(0).start()
 
     def cast_slow(k):
         slow_load(k).wait()
@@ -136,6 +134,9 @@
             ag_copy(j, k, me).start()
 
     cast_slow(0)
+    loop(count, lambda k: slow_load(k).start(), start=1)
+    for i in range(5):
+        load(i).start()
     pl.semaphore_wait(barrier, chips + 1)
 
     def send_slow(k):

time: 149 us -> 85.3 us (0.57)
  Pallas kernels: 142 us -> 78.7 us
    pallas_call x1, Pallas kernels: 142 us -> 78.7 us  [outer_step(): pl.pallas_call(functools.partial(kernel, xor, n, 2 * xor >= n_rep, scale)...]
where the time goes in v1:
time: 85.3 us; the launch traced here: 85.6 us
  Pallas kernels  78.7 us (92%)
  local copies, waits for them, and re-layouts  4.83 us (6%)
  between operations  1.29 us (2%)
    pallas_call x1, Pallas kernels, outer_step(): pl.pallas_call(functools.partial(kernel, xor, n, 2 * xor >= n_rep, scale)...  78.7 us
    unnamed x4, local copies, waits for them, and re-layouts  4.83 us

profile of v1, /device:TPU:0, one launch (start us, length us, event | category | flops | bytes accessed | tf_op | source)
XLA Modules:
  0.0 85.6 jit_solution(5185105965174731328)
XLA Ops:
  1.3 79.5 %conditional.1 = ((bf16[512,768]{1,0:T(8,128)(2,1)S(1)}, bf16[1024,768]{1,0:T(8,128)(2,1)S(1)}, bf16[1024,768]{1,0:T(8,128)(2,1)S(1)}, f32[1024,768]{1,0:T(8,128)S(1)})) conditional(s32[]{:T(128)} %bitcast, (bf16[512,4096]{1,0:T(8,128)(2,1)}, bf16[512,768]{1,0:T(8,128)(2,1)}, bf16[512,768]{1,0:T(8,128)(2,1)}, ...), branch_computations={%region_0.0_spmd, %region_1.0_spmd, %region_2.0_spmd, %region_3.0_... | conditional | flops 6442450944 | bytes 21495816 | solution.py:367
  1.5 78.7 %branch_2_fun.1 = (bf16[512,768]{1,0:T(8,128)(2,1)S(1)}, bf16[1024,768]{1,0:T(8,128)(2,1)S(1)}, bf16[1024,768]{1,0:T(8,128)(2,1)S(1)}, f32[1024,768]{1,0:T(8,128)S(1)}) custom-call(bf16[512,4096]{1,0:T(8,128)(2,1)} %get-tuple-element.135.tok_hbm, bf16[512,768]{1,0:T(8,128)(2,1)} %get-tuple-element.136.gate_hbm, bf16[512,768]{1,0:T(8,128)(2,1)} %get-tuple-element.137.ups_hbm, ...), custom_call_target="tpu_custom_call" | custom-call | flops 6442450944 | bytes 21495808 | tf_op jit(solution)/shard_map/cond/branch_2_fun/pallas_call | solution.py:313
  80.8 1.7 %copy.46 = f32[1,1024,768]{2,1,0:T(8,128)} copy(f32[1,1024,768]{2,1,0:T(8,128)S(1)} %bitcast.8) | data formatting | bytes 6291456
  82.4 1.1 %copy.45 = bf16[1,1024,768]{2,1,0:T(8,128)(2,1)} copy(bf16[1,1024,768]{2,1,0:T(8,128)(2,1)S(1)} %bitcast.10) | data formatting | bytes 3145728
  83.6 0.9 %copy.43 = bf16[512,768]{1,0:T(8,128)(2,1)} copy(bf16[512,768]{1,0:T(8,128)(2,1)S(1)} %get-tuple-element.229) | data formatting | bytes 1572864
  84.4 1.1 %copy.44 = bf16[1,1024,768]{2,1,0:T(8,128)(2,1)} copy(bf16[1,1024,768]{2,1,0:T(8,128)(2,1)S(1)} %bitcast.9) | data formatting | bytes 3145728
